TPU v7x, 256 devices: a whole 4x4x8 slice. The times are simulated.
256 devices in a mesh: chan: 32 (over z, x), slab: 2 (over core), batch: 4 (over y).
Axes of the slice: x: 4, y: 4, z: 8, core: 2. Of those that a mesh axis runs over, the one named last changes fastest.
Arguments:
- inputs: bfloat16 [2048, 8, 512], P(('batch', 'chan'), 'slab'), parts along dimension 0, may hold values from -6 to 6
- weights: bfloat16 [27, 512, 512], P(None, 'chan'), may hold values from -0.09375 to 0.09375
- out_grad: bfloat16 [2048, 8, 512], P(('batch', 'chan'), 'slab'), parts along dimension 0, may hold values from -6 to 6
Outputs:
- conv_out: bfloat16 [2048, 8, 512], P(('batch', 'chan'), 'slab'), parts along dimension 0
- input_grad: bfloat16 [2048, 8, 512], P(('batch', 'chan'), 'slab'), parts along dimension 0
There are 4 independent parts, one for each index of `batch`. A program takes and returns all parts, laid end to end along the dimension named above; an argument that names none is the same for every part. Nothing has to cross between parts.
All inputs are finite; a program needn't handle non-finite values.
Results may differ from a plain program's by a relative error of at most 0.0013.
Values may be sent and summed in bfloat16 or wider, within the bound.
A program may use at most 192 MiB of HBM per device.

v0:
```python
import jax
import jax.numpy as jnp
from jax import lax
from jax.sharding import PartitionSpec as P

NZ = 64


OFFSETS = (-1, 0, 1)


def padded(block, sides, width):
    for axis, dim in sides:
        count = lax.axis_size(axis)
        forward = [(i, i + 1) for i in range(count - 1)]
        forward.append((count - 1, 0))
        backward = [(target, source) for source, target in forward]
        low = lax.ppermute(
            lax.slice_in_dim(block, block.shape[dim] - width, None, axis=dim), axis, forward
        )
        high = lax.ppermute(lax.slice_in_dim(block, 0, width, axis=dim), axis, backward)
        block = jnp.concatenate([low, block, high], axis=dim)
    return block


def stack_yz(block, rows_y):
    chans, slab_len, plane_size = block.shape
    shaped = block.reshape(chans, slab_len, rows_y, NZ)
    pieces = []
    for offset_y in OFFSETS:
        for offset_z in OFFSETS:
            pieces.append(jnp.roll(shaped, (-offset_y, -offset_z), axis=(2, 3)))
    return jnp.stack(pieces).reshape(9 * chans, slab_len * plane_size)


def per_device(inputs, weights, out_grad):
    chans_in, slab_len, plane_size = inputs.shape
    chans_out = out_grad.shape[0]
    full_out = weights.shape[2]
    rows_y = plane_size // NZ
    cell_count = slab_len * plane_size
    halo_in = padded(inputs, (("slab", 1),), 1)
    grad_all = lax.all_gather(out_grad, "chan", axis=0, tiled=True)
    halo_grad = padded(grad_all, (("slab", 1),), 1)
    columns = [
        stack_yz(halo_in[:, 1 + offset_x : 1 + offset_x + slab_len], rows_y) for offset_x in OFFSETS
    ]
    running = jnp.zeros((chans_out * lax.axis_size("chan"), cell_count), jnp.float32)
    for partial_index_x in range(3):
        partial_weight_x = weights[9 * partial_index_x : 9 * partial_index_x + 9]
        partial_weight_x = partial_weight_x.reshape(9 * chans_in, chans_out * lax.axis_size("chan"))
        running = running + lax.dot_general(
            partial_weight_x,
            columns[partial_index_x],
            (((0,), (0,)), ((), ())),
            preferred_element_type=jnp.float32,
        )
    own_rows = lax.psum_scatter(running, "chan", scatter_dimension=0, tiled=True)
    conv_out = own_rows.astype(jnp.bfloat16).reshape(chans_out, slab_len, plane_size)
    running_grad = jnp.zeros((chans_in, slab_len, rows_y, NZ), jnp.float32)
    for index_x, offset_x in enumerate(OFFSETS):
        plane_x = halo_grad[:, 1 - offset_x : 1 - offset_x + slab_len].reshape(full_out, cell_count)
        weight_x = weights[9 * index_x : 9 * index_x + 9].reshape(9 * chans_in, full_out)
        product = lax.dot_general(
            weight_x, plane_x, (((1,), (0,)), ((), ())), preferred_element_type=jnp.float32
        )
        product = product.reshape(9, chans_in, slab_len, rows_y, NZ)
        for index_y, offset_y in enumerate(OFFSETS):
            for index_z, offset_z in enumerate(OFFSETS):
                number = 3 * index_y + index_z
                running_grad = running_grad + jnp.roll(
                    product[number], (offset_y, offset_z), axis=(2, 3)
                )
    input_grad = running_grad.reshape(chans_in, slab_len, plane_size).astype(jnp.bfloat16)
    return (conv_out, input_grad)


def solution(mesh):
    in_specs = (
        P(("batch", "chan"), "slab", None),
        P(None, "chan", None),
        P(("batch", "chan"), "slab", None),
    )
    out_specs = (P(("batch", "chan"), "slab", None), P(("batch", "chan"), "slab", None))
    return jax.shard_map(
        per_device, mesh=mesh, in_specs=in_specs, out_specs=out_specs, check_vma=False
    )
```

profile of v0, /device:TPU:16, one launch (start us, length us, event | category | flops | bytes accessed | tf_op | source)
XLA Modules:
  0.0 322.5 jit_solution(15616600045513753703)
XLA Ops:
  7.9 1.0 fusion.86
  9.5 1.0 reshape.140
  10.6 1.1 fusion.31
  11.7 0.9 fusion.32
  14.4 1.1 fusion.57
  16.4 0.9 reshape.141
  17.3 2.7 fusion.88
  23.0 0.9 reshape.144
  26.1 0.9 reshape.138
  27.8 1.4 copy-done.1
  29.2 2.8 add_bitcast_fusion
  32.1 5.4 %copy.11 = f32[512,2048]{1,0:T(8,128)} copy(f32[512,2048]{0,1:T(8,128)} %add_bitcast_fusion) | data formatting | bytes 8388608
  37.5 53.8 %all-gather.2.cloned.1.call-done = bf16[512,4,512]{2,1,0:T(4,128)(2,1)} async-done(((bf16[16,4,512]{2,1,0:T(4,128)(2,1)}), bf16[512,4,512]{2,1,0:T(4,128)(2,1)}) %all-gather.2.cloned.1.call-update) | async-done | bytes 2097168 | tf_op jit(solution)/shard_map/all_gather | solution.py:43
  91.3 2.2 copy.14
  94.0 0.9 fusion.71
  95.9 1.5 fusion.69
  97.4 1.0 copy.6
  98.4 0.9 copy.8
  99.9 1.0 squeeze.98
  101.2 0.9 fusion.7
  103.2 0.9 fusion.4
  104.1 1.0 squeeze.91
  114.0 1.9 copy.7
  115.9 1.9 copy.9
  117.7 5.6 %pad_maximum_fusion.1 = (bf16[512,4,512]{2,1,0:T(4,128)(2,1)S(1)}, bf16[512,4,512]{2,1,0:T(4,128)(2,1)}) fusion(bf16[512,1,512]{2,1,0:T(2,128)(2,1)S(1)} %copy.7, bf16[512,4,512]{2,1,0:T(4,128)(2,1)S(1)} %copy-done, bf16[512,1,512]{2,1,0:T(2,128)(2,1)S(1)} %copy.9), kind=kLoop, calls=%fused_computation.4 | loop fusion | flops 8388608 | bytes 7340032 | tf_op jit(solution)/shard_map/concatenate | solution.py:22
  124.5 1.0 fusion.70
  128.3 0.9 fusion.72
  139.5 1.0 squeeze.103
  140.5 1.0 squeeze.85
  141.6 1.0 add_convert_fusion
  142.6 171.1 %reduce-scatter.4.cloned.1.call-done = f32[16,2048]{1,0:T(8,128)} async-done(((f32[512,2048]{1,0:T(8,128)}), f32[16,2048]{1,0:T(8,128)}) %reduce-scatter.4.cloned.1.call-update) | async-done | bytes 131088
  313.7 1.2 copy.12
  (251 shorter events, 36.7 us)
Async XLA Ops:
  7.2 84.1 %all-gather.2.cloned.1.call-start = ((), (), s32[]{:S(2)}) async-start(), calls=%async_computation.1 | async-start | bytes 2162688 | tf_op jit(solution)/shard_map/all_gather | solution.py:43
  7.9 305.8 %reduce-scatter.4.cloned.1.call-start = ((), (), s32[]{:S(2)}) async-start(), calls=%async_computation.2 | async-start | bytes 4325376
  8.9 11.1 %collective-permute-start = (bf16[16,1,512]{2,1,0:T(2,128)(2,1)S(1)}, bf16[16,1,512]{2,1,0:T(2,128)(2,1)S(1)}, u32[]{:S(2)}, u32[]{:S(2)}) collective-permute-start(bf16[16,1,512]{2,1,0:T(2,128)(2,1)S(1)} %get-tuple-element.91), channel_id=1, source_target_pairs={{0,4},{4,0},{1,5},{5,1},{2,6},{6,2},{3,7},{7,3},{8,12},{12,8},{9,1... | collective-permute-start | bytes 49160 | tf_op jit(solution)/shard_map/ppermute | solution.py:18
  9.0 11.0 %collective-permute-start.1 = (bf16[16,1,512]{2,1,0:T(2,128)(2,1)S(1)}, bf16[16,1,512]{2,1,0:T(2,128)(2,1)S(1)}, u32[]{:S(2)}, u32[]{:S(2)}) collective-permute-start(bf16[16,1,512]{2,1,0:T(2,128)(2,1)S(1)} %get-tuple-element.90), channel_id=1, source_target_pairs={{4,0},{0,4},{5,1},{1,5},{6,2},{2,6},{7,3},{3,7},{12,8},{8,12},{13,... | collective-permute-start | bytes 49160 | tf_op jit(solution)/shard_map/ppermute | solution.py:21
  10.6 2.9 copy-start.7
  11.7 2.6 copy-start.33
  13.5 2.2 copy-start.31
  14.3 1.5 copy-start.32
  27.0 2.2 copy-start.1
  94.0 1.9 copy-start
  98.3 1.5 copy-start.28
  98.3 15.6 %collective-permute-start.2 = (bf16[512,1,512]{2,0,1:T(8,128)(2,1)}, bf16[512,1,512]{2,0,1:T(8,128)(2,1)}, u32[]{:S(2)}, u32[]{:S(2)}) collective-permute-start(bf16[512,1,512]{2,0,1:T(8,128)(2,1)} %copy.6), channel_id=1, source_target_pairs={{4,0},{0,4},{5,1},{1,5},{6,2},{2,6},{7,3},{3,7},{12,8},{8,12},{13,... | collective-permute-start | bytes 1572872 | tf_op jit(solution)/shard_map/ppermute | solution.py:21
  99.3 16.6 %collective-permute-start.3 = (bf16[512,1,512]{2,0,1:T(8,128)(2,1)}, bf16[512,1,512]{2,0,1:T(8,128)(2,1)}, u32[]{:S(2)}, u32[]{:S(2)}) collective-permute-start(bf16[512,1,512]{2,0,1:T(8,128)(2,1)} %copy.8), channel_id=1, source_target_pairs={{0,4},{4,0},{1,5},{5,1},{2,6},{6,2},{3,7},{7,3},{8,12},{12,8},{9,1... | collective-permute-start | bytes 1572872 | tf_op jit(solution)/shard_map/ppermute | solution.py:18
  102.9 2.9 copy-start.5
  105.8 2.4 copy-start.6
  106.7 2.4 copy-start.8
  107.4 2.4 copy-start.25
  109.1 2.0 copy-start.24
  110.3 2.0 copy-start.21
  111.3 1.9 copy-start.30
  125.5 1.6 copy-start.2
  129.2 1.0 copy-start.27
  130.2 1.0 copy-start.4
  138.9 2.6 copy-start.9
  139.0 2.6 copy-start.10
  139.0 2.6 copy-start.11
  139.0 2.6 copy-start.12
  139.0 2.6 copy-start.13
  139.0 2.6 copy-start.14
  139.0 2.6 copy-start.15
  139.0 2.6 copy-start.16
  139.0 2.6 copy-start.29
  (13 other events, 11.4 us)
Sparse Core Ops, SparseCore 0:
  10.6 80.6 all-gather.1
  95.2 218.4 reduce-scatter.3
where the time goes:
time: 323 us
  waiting for transfers between devices  226 us (70%)
  local copies, waits for them, and re-layouts  50.9 us (16%)
  other arithmetic  22 us (7%)
  between operations  15.1 us (5%)
  matrix products  7.78 us (2%)
    unnamed x3, waiting for transfers between devices  172 us
    all_gather x1, waiting for transfers between devices, per_device(): grad_all = lax.all_gather(out_grad, 'chan', axis=0, tiled=True)  53.8 us
    unnamed x83, local copies, waits for them, and re-layouts  14.6 us
    concatenate x20, local copies, waits for them, and re-layouts, per_device(): jnp.roll(product[number], (offset_y, offset_z), axis=(2, 3))  7.88 us
    squeeze x27, local copies, waits for them, and re-layouts, per_device(): product[number]  7 us
    concatenate x32, other arithmetic, per_device(): jnp.roll(product[number], (offset_y, offset_z), axis=(2, 3))  6.98 us
  transfers between devices with their start and end apart: 6, of which 2 were waited for; matrix products, arithmetic and copies ran while one was open for 23% of the time, Pallas kernels for 0%

commit v1 on v0

v1 whole, which is shorter than its diff:
```python
import jax
import jax.numpy as jnp
from jax import lax
from jax.experimental import pallas as pl
from jax.experimental.pallas import tpu as pltpu
from jax.sharding import PartitionSpec as P

BF = jnp.bfloat16
F32 = jnp.float32
MESH = pl.DeviceIdType.MESH
NXC = 4
NZC = 8


def remote(src, dst, send, recv, chan, slab):
    return pltpu.make_async_remote_copy(
        src_ref=src,
        dst_ref=dst,
        send_sem=send,
        recv_sem=recv,
        device_id={"chan": chan, "slab": slab},
        device_id_type=MESH,
    )


def arrived(ref, sem):
    pltpu.make_async_copy(ref, ref, sem).wait()


def iota(shape, dim):
    return lax.broadcasted_iota(jnp.int32, shape, dim)


def kernel(
    g_ref, x_ref, w_ref, go_ref, co_ref,
    perm, permw, part, acts, wl, wpack, wrecv, wfwd, wbwd, outs, outr, hprod,
    loc_sem, xs, xr, zs, zr, ss, sr, ws, wr, fs, fr, bs, br, bx, by, os_, or_,
):
    chan = lax.axis_index("chan")
    s = lax.axis_index("slab")
    z = chan // NXC
    x = chan % NXC
    sib = 1 - s

    def at(zz, xx):
        return lax.rem(zz + 2 * NZC, NZC) * NXC + lax.rem(xx + 2 * NXC, NXC)

    barrier = pltpu.get_barrier_semaphore()
    peers = [(at(z, x), sib)]
    for k in range(1, NXC):
        peers += [(at(z, x + k), s), (at(z, x + k), sib)]
    for k in range(1, NZC):
        peers.append((at(z + k, x), s))
    for c, d in peers:
        pl.semaphore_signal(
            barrier, inc=1, device_id={"chan": c, "slab": d}, device_id_type=MESH
        )

    n = iota((1, 512), 1)
    quarter, yy, zz = n // 128, (n % 128) // 16, n % 16
    main_src = yy * 64 + quarter * 16 + zz
    halo_src = yy * 64 + (quarter * 16 + jnp.where(zz < 8, -1, 16) + 64) % 64
    m = iota((512, 512), 0)
    perm[:, 0:512] = (m == main_src).astype(F32).astype(BF)
    perm[:, 512:1024] = (m == halo_src).astype(F32).astype(BF)

    lane = iota((16, 128), 1)
    halo = [jnp.zeros((16, 128), F32) for _ in range(NXC)]
    for t, ref in ((0, g_ref), (1, x_ref)):
        moved = jnp.dot(ref[...], perm[...], preferred_element_type=F32)
        for p in range(4):
            keep = lane % 8 == (s + t) % 2 * 4 + p
            for q in range(NXC):
                rows = moved[16 * p : 16 * p + 16]
                part[q, 5 * t + p] = rows[:, 128 * q : 128 * q + 128].astype(BF)
                halo[q] = halo[q] + jnp.where(
                    keep, rows[:, 512 + 128 * q : 640 + 128 * q], 0.0
                )
    for q in range(NXC):
        part[q, 4] = halo[q].astype(BF)

    pl.semaphore_wait(barrier, len(peers))

    my_rows = pl.ds(pl.multiple_of(chan * 16, 16), 16)
    span = (pl.ds(0, 5), pl.ds(5, 4))
    waits = []
    own = pltpu.make_async_copy(part.at[x], acts.at[s, :, my_rows], loc_sem.at[0])
    own.start()
    for i in range(2):
        for k in (1, 3, 2):
            dest = lax.rem(x + k, NXC)
            copy = remote(
                part.at[dest, span[i]], acts.at[s, span[i], my_rows],
                xs.at[k - 1, i], xr.at[k - 1, i], at(z, dest), s,
            )
            copy.start()
            waits.append(copy)

    half = pl.ds(pl.multiple_of(s * 256, 128), 256)
    low = pl.ds(pl.multiple_of(s * 256, 128), 128)
    high = pl.ds(pl.multiple_of(s * 256 + 128, 128), 128)

    def wrow(k):
        return pl.ds(pl.multiple_of(lax.rem(x + k + NXC, NXC) * 16, 16), 16)

    own_w = pltpu.make_async_copy(
        w_ref.at[:, :, half], wbwd.at[:, wrow(0), half], loc_sem.at[1]
    )
    own_w.start()
    for i, k in enumerate((1, -1)):
        copy = remote(
            w_ref.at[:, :, half], wbwd.at[:, wrow(0), half],
            bs.at[i], br.at[i], at(z, x + k), s,
        )
        copy.start()
        waits.append(copy)

    n = iota((1, 256), 1)
    v, j, c = n // 128, (n % 128) // 32, n % 32
    permw[...] = (iota((512, 256), 0) == j * 128 + (2 * v + s) * 32 + c).astype(F32).astype(BF)
    for o in range(28):
        for t in range(4):
            at_rows, at_lanes = pl.ds(o // 4 * 16, 16), pl.ds(o % 4 * 128, 128)
            if o < 27:
                wl[t, at_rows, at_lanes] = w_ref[o, :, 128 * t : 128 * t + 128]
            else:
                wl[t, at_rows, at_lanes] = jnp.zeros((16, 128), BF)
    for t in range(4):
        packed = jnp.dot(wl[t], permw[...], preferred_element_type=F32).astype(BF)
        for v in range(2):
            for g in range(7):
                wpack[2 * t + v, g] = packed[16 * g : 16 * g + 16, 128 * v : 128 * v + 128]
    own_f = pltpu.make_async_copy(wpack.at[z], wrecv.at[:, z, x], loc_sem.at[2])
    own_f.start()
    for k in (4, 3, 5, 2, 6, 1, 7):
        dest = lax.rem(z + k, NZC)
        copy = remote(
            wpack.at[dest], wrecv.at[:, z, x], ws.at[k - 1], wr.at[k - 1], at(dest, x), s
        )
        copy.start()
        waits.append(copy)

    def block(k):
        return pl.ds(pl.multiple_of(lax.rem(z + k + NZC, NZC) * 64, 64), 64)

    def pass_on(k, i, direction, hop):
        ref = acts.at[s, span[i], block(k)]
        if direction is not None:
            step = 1 if direction == 0 else -1
            copy = remote(
                ref, ref, zs.at[direction, hop, i], zr.at[direction, hop, i],
                at(z + step, x), s,
            )
            copy.start()
            waits.append(copy)
        return ref

    def to_sibling(k, i):
        ref = acts.at[s, span[i], block(k)]
        copy = remote(
            ref, ref, ss.at[(k + NZC) % NZC, i], sr.at[(k + NZC) % NZC, i], at(z, x), sib
        )
        copy.start()
        waits.append(copy)

    own.wait()
    for i in range(2):
        for k in (1, 3, 2):
            source = lax.rem(x - k + NXC, NXC)
            rows = pl.ds(pl.multiple_of((z * NXC + source) * 16, 16), 16)
            arrived(acts.at[s, span[i], rows], xr.at[k - 1, i])
        pass_on(0, i, 0, 0)
        pass_on(0, i, 1, 0)
        to_sibling(0, i)

    def hop(h):
        for i in range(2):
            for direction in range(2):
                if h == 4 and i != direction:
                    continue
                k = -h if direction == 0 else h
                ref = acts.at[s, span[i], block(k)]
                arrived(ref, zr.at[direction, h - 1, i])
                if h < 3 or (h == 3 and i == direction):
                    pass_on(k, i, direction, h)
                to_sibling(k, i)

    hop(1)

    own_w.wait()
    for i, (k, to, lanes) in enumerate(((-1, 1, low), (1, -1, high))):
        arrived(wbwd.at[:, wrow(k), half], br.at[i])
        copy = remote(
            wbwd.at[:, wrow(k), lanes], wbwd.at[:, wrow(k), lanes],
            bs.at[2 + i], br.at[2 + i], at(z, x + to), s,
        )
        copy.start()
        waits.append(copy)

    own_f.wait()
    for k in range(1, NZC):
        source = lax.rem(z - k + NZC, NZC)
        arrived(wrecv.at[:, source, x], wr.at[k - 1])
    for i, k in enumerate((1, -1)):
        ref = wrecv.at[:, :, x]
        copy = remote(ref, ref, fs.at[i], fr.at[i], at(z, x + k), s)
        copy.start()
        waits.append(copy)

    hop(2)

    for i, (k, to) in enumerate(((-1, 1), (1, -1))):
        source = lax.rem(x + k + NXC, NXC)
        arrived(wrecv.at[:, :, source], fr.at[i])
        ref = wrecv.at[:, pl.ds(4 * i, 4), source]
        copy = remote(ref, ref, fs.at[2 + i], fr.at[2 + i], at(z, x + to), s)
        copy.start()
        waits.append(copy)
    for i, lanes in enumerate((low, high)):
        arrived(wbwd.at[:, wrow(2), lanes], br.at[2 + i])
    theirs = pl.ds(pl.multiple_of(sib * 32, 32), 32)
    mine = pl.ds(pl.multiple_of(s * 32, 32), 32)
    swap = remote(
        wbwd.at[:, theirs, half], wbwd.at[:, theirs, half], bx.at[0], by.at[0], at(z, x), sib
    )
    swap.start()
    waits.append(swap)

    hop(3)
    hop(4)

    other = pl.ds(pl.multiple_of(sib * 256, 128), 256)
    arrived(wbwd.at[:, mine, other], by.at[0])
    for i in range(2):
        for k in range(NZC):
            arrived(acts.at[sib, span[i], block(k)], sr.at[k, i])

    lane_z = iota((32, 128), 1) % 16
    lane_k = iota((512, 128), 1) % 8

    def conv(weights_of, t):
        sign = 1 if t == 0 else -1
        first, second = (0, 1) if t == 0 else (1, 0)
        edge = jnp.where(lane_k < 4, acts[first, 4], acts[second, 4])
        for ai in range(3):
            hprod[ai] = jnp.dot(weights_of(ai), edge, preferred_element_type=F32)

        def over_y(read, ci):
            total = read(3 + ci)
            for bi in (0, 2):
                shift = (16 * (bi - 1) * sign) % 128
                total = total + pltpu.roll(read(3 * bi + ci), shift, 1)
            return total

        edges = {}
        for ai in range(3):
            for ci in (0, 2):
                edges[ai, ci] = over_y(lambda r: hprod[ai, 32 * r : 32 * r + 32], ci)
        for pair in range(4):
            total = None
            for ai in range(3):
                planes = [(2 * pair + i - sign * (ai - 1)) % 8 for i in range(2)]
                both = jnp.concatenate(
                    [acts[p // 4, 5 * t + p % 4] for p in planes], axis=1
                )
                term = jnp.dot(weights_of(ai), both, preferred_element_type=F32)
                total = term if total is None else total + term
            for i in range(2):
                plane = 2 * pair + i
                cells = total[:, 128 * i : 128 * i + 128]

                def read(r):
                    return cells[32 * r : 32 * r + 32]

                result = over_y(read, 1)
                for ci in (0, 2):
                    e = sign * (ci - 1)
                    moved = pltpu.roll(over_y(read, ci), e % 128, 1)
                    outside = None
                    for ai in range(3):
                        source = (plane - sign * (ai - 1) + 4 * t) % 8
                        shift = (-source if e == 1 else 7 - source) % 128
                        term = edges[ai, ci]
                        if shift:
                            term = pltpu.roll(term, shift, 1)
                        outside = term if outside is None else outside + term
                    border = lane_z == (0 if e == 1 else 15)
                    result = result + jnp.where(border, outside, moved)
                result = result.astype(BF)
                for j in range(2):
                    outs[t, j, plane] = result[16 * j : 16 * j + 16]

        for j in range(2):
            for to in range(2):
                owner = 2 * s + j
                src = outs.at[t, j, pl.ds(4 * to, 4)]
                dst = outr.at[t, x]
                itself = jnp.logical_and(owner == x, s == to)

                @pl.when(itself)
                def _():
                    pltpu.make_async_copy(src, dst, or_.at[t, x]).start()

                @pl.when(jnp.logical_not(itself))
                def _():
                    remote(
                        src, dst, os_.at[t, j, to], or_.at[t, x], at(z, owner), to
                    ).start()

    def bwd_rows(ai):
        return wbwd[9 * ai : 9 * ai + 9, mine, :].reshape(288, 512)

    conv(bwd_rows, 0)

    for i in range(2):
        source = lax.rem(x + 2, NXC)
        arrived(wrecv.at[:, pl.ds(4 * i, 4), source], fr.at[2 + i])
    for g in range(7):
        wfwd[128 * g : 128 * g + 128, :] = wrecv[g].reshape(512, 128).T

    conv(lambda ai: wfwd[288 * ai : 288 * ai + 288, :], 1)

    for t, ref in ((0, go_ref), (1, co_ref)):
        for q in range(NXC):
            arrived(outr.at[t, q], or_.at[t, q])
        joined = jnp.concatenate(
            [outr[t, q].reshape(64, 128) for q in range(NXC)], axis=1
        )
        ref[...] = lax.dot_general(
            joined, perm[:, 0:512], (((1,), (1,)), ((), ())), preferred_element_type=F32
        ).astype(BF)

    for copy in waits:
        copy.wait_send()
    for t in range(2):
        for j in range(2):
            for to in range(2):
                owner = 2 * s + j

                @pl.when(jnp.logical_not(jnp.logical_and(owner == x, s == to)))
                def _():
                    remote(
                        outs.at[t, j, pl.ds(4 * to, 4)], outr.at[t, x],
                        os_.at[t, j, to], or_.at[t, x], at(z, owner), to,
                    ).wait_send()


def per_device(inputs, weights, out_grad):
    chans, slab_len, plane_size = inputs.shape

    def rows(block):
        return block.transpose(1, 0, 2).reshape(slab_len * chans, plane_size)

    vmem = pl.BlockSpec(memory_space=pltpu.VMEM)
    shape = jax.ShapeDtypeStruct((slab_len * chans, plane_size), BF)
    dma = pltpu.SemaphoreType.DMA
    grad, conv = pl.pallas_call(
        kernel,
        out_shape=(shape, shape),
        in_specs=[vmem] * 3,
        out_specs=(vmem, vmem),
        scratch_shapes=[
            pltpu.VMEM((512, 1024), BF),
            pltpu.VMEM((512, 256), BF),
            pltpu.VMEM((4, 9, 16, 128), BF),
            pltpu.VMEM((2, 9, 512, 128), BF),
            pltpu.VMEM((4, 112, 512), BF),
            pltpu.VMEM((8, 7, 16, 128), BF),
            pltpu.VMEM((7, 8, 4, 16, 128), BF),
            pltpu.VMEM((896, 512), BF),
            pltpu.VMEM((27, 64, 512), BF),
            pltpu.VMEM((2, 2, 8, 16, 128), BF),
            pltpu.VMEM((2, 4, 4, 16, 128), BF),
            pltpu.VMEM((3, 288, 128), F32),
            dma((3,)),
            dma((3, 2)), dma((3, 2)),
            dma((2, 4, 2)), dma((2, 4, 2)),
            dma((8, 2)), dma((8, 2)),
            dma((7,)), dma((7,)),
            dma((4,)), dma((4,)),
            dma((4,)), dma((4,)),
            dma((1,)), dma((1,)),
            dma((2, 2, 2)), dma((2, 4)),
        ],
        compiler_params=pltpu.CompilerParams(
            collective_id=0, has_side_effects=True, vmem_limit_bytes=48 * 1024 * 1024
        ),
    )(rows(out_grad), rows(inputs), weights)

    def back(block):
        return block.reshape(slab_len, chans, plane_size).transpose(1, 0, 2)

    return back(conv), back(grad)


def solution(mesh):
    act = P(("batch", "chan"), "slab", None)
    return jax.shard_map(
        per_device,
        mesh=mesh,
        in_specs=(act, P(None, "chan", None), act),
        out_specs=(act, act),
        check_vma=False,
    )
```

time: 323 us -> 44.7 us (0.14)
  the two profiles are of different devices: /device:TPU:16 before, /device:TPU:1 now
where the time goes in v1:
time: 44.7 us; the launch traced here: 44.6 us
  Pallas kernels  41.2 us (92%)
  local copies, waits for them, and re-layouts  2.67 us (6%)
  between operations  0.67 us (1%)
    pallas_call x1, Pallas kernels, per_device(): pl.pallas_call(kernel, out_shape=(shape, shape), in_specs=[vmem] * 3, out...  41.2 us
    unnamed x4, local copies, waits for them, and re-layouts  1.01 us
    transpose x2, local copies, waits for them, and re-layouts, rows(): return block.transpose(1, 0, 2).reshape(slab_len * chans, plane_size)  0.9 us

profile of v1, /device:TPU:1, one launch (start us, length us, event | category | flops | bytes accessed | tf_op | source)
XLA Modules:
  0.0 44.6 jit_solution(15966722489285585130)
XLA Ops:
  0.6 0.0 copy-start.1
  0.6 0.9 %copy.6 = bf16[4,16,512]{2,1,0:T(8,128)(2,1)S(1)} copy(bf16[4,16,512]{2,0,1:T(4,128)(2,1)} %bitcast.14) | data formatting | bytes 131072 | tf_op jit(solution)/shard_map/transpose | solution.py:352
  1.5 0.0 copy-done.1
  1.6 0.0 copy-start
  1.6 1.0 %copy-done = bf16[27,16,512]{2,1,0:T(8,128)(2,1)S(1)} copy-done((bf16[27,16,512]{2,1,0:T(8,128)(2,1)S(1)}, bf16[27,16,512]{2,1,0:T(8,128)(2,1)}, u32[]{:S(2)}) %copy-start) | copy-done | bytes 442392
  2.6 41.2 %shard_map.50 = (bf16[64,512]{1,0:T(8,128)(2,1)S(1)}, bf16[64,512]{1,0:T(8,128)(2,1)S(1)}) custom-call(bf16[64,512]{1,0:T(8,128)(2,1)S(1)} %bitcast.11, bf16[64,512]{1,0:T(8,128)(2,1)S(1)} %bitcast.10, bf16[27,16,512]{2,1,0:T(8,128)(2,1)S(1)} %copy-done), custom_call_target="tpu_custom_call" | custom-call | tf_op jit(solution)/shard_map/pallas_call | solution.py:357
  43.8 0.8 %copy_bitcast_fusion = (bf16[16,4,512]{2,1,0:T(4,128)(2,1)}, bf16[16,4,512]{2,1,0:T(4,128)(2,1)}) fusion(bf16[4,16,512]{2,1,0:T(8,128)(2,1)S(1)} %bitcast.12, bf16[4,16,512]{2,1,0:T(8,128)(2,1)S(1)} %bitcast.13), kind=kLoop, calls=%fused_computation | loop fusion | bytes 262144 | tf_op jit(solution)/shard_map/transpose | solution.py:391
  (1 shorter events, 0.0 us)
Async XLA Ops:
  0.6 0.9 %copy-start.1 = (bf16[16,4,512]{2,1,0:T(4,128)(2,1)S(1)}, bf16[16,4,512]{2,1,0:T(4,128)(2,1)}, u32[]{:S(2)}) copy-start(bf16[16,4,512]{2,1,0:T(4,128)(2,1)} %param.5) | copy-start | bytes 196612
  1.6 1.0 %copy-start = (bf16[27,16,512]{2,1,0:T(8,128)(2,1)S(1)}, bf16[27,16,512]{2,1,0:T(8,128)(2,1)}, u32[]{:S(2)}) copy-start(bf16[27,16,512]{2,1,0:T(8,128)(2,1)} %w_ref.1) | copy-start | bytes 1327108

commit v2 on v1

--- a/solution.py
+++ b/solution.py
@@ -9,16 +9,20 @@
 F32 = jnp.float32
 MESH = pl.DeviceIdType.MESH
 NXC = 4
+NYC = 4
 NZC = 8
 
 
-def remote(src, dst, send, recv, chan, slab):
+def remote(src, dst, send, recv, chan, slab, batch=None):
+    where = {"chan": chan, "slab": slab}
+    if batch is not None:
+        where["batch"] = batch
     return pltpu.make_async_remote_copy(
         src_ref=src,
         dst_ref=dst,
         send_sem=send,
         recv_sem=recv,
-        device_id={"chan": chan, "slab": slab},
+        device_id=where,
         device_id_type=MESH,
     )
 
@@ -32,15 +36,28 @@
 
 
 def kernel(
-    g_ref, x_ref, w_ref, go_ref, co_ref,
+    g_hbm, x_hbm, w_hbm, go_ref, co_ref,
+    raw, tall, w_ref, in_sem,
     perm, permw, part, acts, wl, wpack, wrecv, wfwd, wbwd, outs, outr, hprod,
-    loc_sem, xs, xr, zs, zr, ss, sr, ws, wr, fs, fr, bs, br, bx, by, os_, or_,
+    loc_sem, xs, xr, zs, zr, ss, sr, ws, wr, fs, fr, fs2, fr2, yfs, yfr,
+    bs, br, bs2, br2, ybs, ybr, bx, by, os_, or_,
 ):
+    fetch = [
+        pltpu.make_async_copy(src, dst, in_sem.at[i])
+        for i, (src, dst) in enumerate(
+            ((g_hbm, raw.at[0]), (x_hbm, raw.at[1]), (w_hbm, w_ref))
+        )
+    ]
+    for copy in fetch:
+        copy.start()
     chan = lax.axis_index("chan")
     s = lax.axis_index("slab")
     z = chan // NXC
     x = chan % NXC
+    y = lax.axis_index("batch")
     sib = 1 - s
+    par = lax.rem(y, 2)
+    y_next = (lax.rem(y + 1, NYC), lax.rem(y + NYC - 1, NYC))
 
     def at(zz, xx):
         return lax.rem(zz + 2 * NZC, NZC) * NXC + lax.rem(xx + 2 * NXC, NXC)
@@ -55,6 +72,11 @@
         pl.semaphore_signal(
             barrier, inc=1, device_id={"chan": c, "slab": d}, device_id_type=MESH
         )
+    for b in y_next:
+        pl.semaphore_signal(
+            barrier, inc=1, device_id={"chan": chan, "slab": s, "batch": b},
+            device_id_type=MESH,
+        )
 
     n = iota((1, 512), 1)
     quarter, yy, zz = n // 128, (n % 128) // 16, n % 16
@@ -66,8 +88,22 @@
 
     lane = iota((16, 128), 1)
     halo = [jnp.zeros((16, 128), F32) for _ in range(NXC)]
-    for t, ref in ((0, g_ref), (1, x_ref)):
-        moved = jnp.dot(ref[...], perm[...], preferred_element_type=F32)
+    for t in range(2):
+        fetch[t].wait()
+        for i in range(16):
+            for v in range(4):
+                tall[4 * t + v, 4 * i : 4 * i + 4] = raw[
+                    t, i, :, 128 * v : 128 * v + 128
+                ].astype(F32)
+        planes = [
+            jnp.concatenate(
+                [tall[4 * t + v, pl.ds(p, 16, stride=4)] for v in range(4)], axis=1
+            )
+            for p in range(4)
+        ]
+        moved = jnp.dot(
+            jnp.concatenate(planes, axis=0).astype(BF), perm[...], preferred_element_type=F32
+        )
         for p in range(4):
             keep = lane % 8 == (s + t) % 2 * 4 + p
             for q in range(NXC):
@@ -79,10 +115,11 @@
     for q in range(NXC):
         part[q, 4] = halo[q].astype(BF)
 
-    pl.semaphore_wait(barrier, len(peers))
+    pl.semaphore_wait(barrier, len(peers) + 2)
 
     my_rows = pl.ds(pl.multiple_of(chan * 16, 16), 16)
     span = (pl.ds(0, 5), pl.ds(5, 4))
+    chunk = (pl.ds(0, 2), pl.ds(2, 3), pl.ds(5, 2), pl.ds(7, 2))
     waits = []
     own = pltpu.make_async_copy(part.at[x], acts.at[s, :, my_rows], loc_sem.at[0])
     own.start()
@@ -97,21 +134,30 @@
             waits.append(copy)
 
     half = pl.ds(pl.multiple_of(s * 256, 128), 256)
-    low = pl.ds(pl.multiple_of(s * 256, 128), 128)
-    high = pl.ds(pl.multiple_of(s * 256 + 128, 128), 128)
+    here = pl.ds(pl.multiple_of(s * 256 + par * 128, 128), 128)
+    there = pl.ds(pl.multiple_of(s * 256 + (1 - par) * 128, 128), 128)
+    offsets = (pl.ds(0, 14), pl.ds(14, 13))
 
     def wrow(k):
         return pl.ds(pl.multiple_of(lax.rem(x + k + NXC, NXC) * 16, 16), 16)
 
+    fetch[2].wait()
     own_w = pltpu.make_async_copy(
         w_ref.at[:, :, half], wbwd.at[:, wrow(0), half], loc_sem.at[1]
     )
     own_w.start()
-    for i, k in enumerate((1, -1)):
-        copy = remote(
-            w_ref.at[:, :, half], wbwd.at[:, wrow(0), half],
-            bs.at[i], br.at[i], at(z, x + k), s,
-        )
+    for h in range(2):
+        for i, k in enumerate((1, -1)):
+            copy = remote(
+                w_ref.at[offsets[h], :, here], wbwd.at[offsets[h], wrow(0), here],
+                bs.at[i, h], br.at[i, h], at(z, x + k), s,
+            )
+            copy.start()
+            waits.append(copy)
+
+    def w_along_y(j, k, h):
+        ref = wbwd.at[offsets[h], wrow(k), here]
+        copy = remote(ref, ref, ybs.at[j, h], ybr.at[j, h], chan, s, y_next[h])
         copy.start()
         waits.append(copy)
 
@@ -130,30 +176,45 @@
         for v in range(2):
             for g in range(7):
                 wpack[2 * t + v, g] = packed[16 * g : 16 * g + 16, 128 * v : 128 * v + 128]
-    own_f = pltpu.make_async_copy(wpack.at[z], wrecv.at[:, z, x], loc_sem.at[2])
-    own_f.start()
-    for k in (4, 3, 5, 2, 6, 1, 7):
+    zmine = lax.rem(z, 2) == par
+
+    def own_forward():
+        return pltpu.make_async_copy(
+            wpack.at[z], wrecv.at[:, z // 2, par, x], loc_sem.at[2]
+        )
+
+    def to_z(k):
         dest = lax.rem(z + k, NZC)
-        copy = remote(
-            wpack.at[dest], wrecv.at[:, z, x], ws.at[k - 1], wr.at[k - 1], at(dest, x), s
-        )
+        return remote(
+            wpack.at[dest], wrecv.at[:, z // 2, par, x], ws.at[k - 1], wr.at[k - 1],
+            at(dest, x), s,
+        )
+
+    @pl.when(zmine)
+    def _():
+        own_forward().start()
+        for k in (4, 3, 5, 2, 6, 1, 7):
+            to_z(k).start()
+
+    pairs = (pl.ds(0, 2), pl.ds(2, 2))
+
+    def f_along_y(j, k, h):
+        ref = wrecv.at[:, pairs[h], par, lax.rem(x + k + NXC, NXC)]
+        copy = remote(ref, ref, yfs.at[j, h], yfr.at[j, h], chan, s, y_next[h])
         copy.start()
         waits.append(copy)
 
     def block(k):
         return pl.ds(pl.multiple_of(lax.rem(z + k + NZC, NZC) * 64, 64), 64)
 
-    def pass_on(k, i, direction, hop):
-        ref = acts.at[s, span[i], block(k)]
-        if direction is not None:
-            step = 1 if direction == 0 else -1
-            copy = remote(
-                ref, ref, zs.at[direction, hop, i], zr.at[direction, hop, i],
-                at(z + step, x), s,
-            )
-            copy.start()
-            waits.append(copy)
-        return ref
+    def pass_on(k, c, direction, hop):
+        ref = acts.at[s, chunk[c], block(k)]
+        copy = remote(
+            ref, ref, zs.at[direction, hop, c], zr.at[direction, hop, c],
+            at(z + (1 if direction == 0 else -1), x), s,
+        )
+        copy.start()
+        waits.append(copy)
 
     def to_sibling(k, i):
         ref = acts.at[s, span[i], block(k)]
@@ -169,55 +230,76 @@
             source = lax.rem(x - k + NXC, NXC)
             rows = pl.ds(pl.multiple_of((z * NXC + source) * 16, 16), 16)
             arrived(acts.at[s, span[i], rows], xr.at[k - 1, i])
-        pass_on(0, i, 0, 0)
-        pass_on(0, i, 1, 0)
+        for c in (2 * i, 2 * i + 1):
+            pass_on(0, c, 0, 0)
+            pass_on(0, c, 1, 0)
         to_sibling(0, i)
 
     def hop(h):
-        for i in range(2):
+        for c in range(4):
             for direction in range(2):
-                if h == 4 and i != direction:
+                if h == 4 and c // 2 != direction:
                     continue
                 k = -h if direction == 0 else h
-                ref = acts.at[s, span[i], block(k)]
-                arrived(ref, zr.at[direction, h - 1, i])
-                if h < 3 or (h == 3 and i == direction):
-                    pass_on(k, i, direction, h)
-                to_sibling(k, i)
-
-    hop(1)
+                arrived(acts.at[s, chunk[c], block(k)], zr.at[direction, h - 1, c])
+                if h < 3 or (h == 3 and c // 2 == direction):
+                    pass_on(k, c, direction, h)
+                if c % 2:
+                    to_sibling(k, c // 2)
 
     own_w.wait()
-    for i, (k, to, lanes) in enumerate(((-1, 1, low), (1, -1, high))):
-        arrived(wbwd.at[:, wrow(k), half], br.at[i])
-        copy = remote(
-            wbwd.at[:, wrow(k), lanes], wbwd.at[:, wrow(k), lanes],
-            bs.at[2 + i], br.at[2 + i], at(z, x + to), s,
-        )
-        copy.start()
-        waits.append(copy)
-
-    own_f.wait()
+    for h in range(2):
+        for i, (k, to) in enumerate(((-1, 1), (1, -1))):
+            ref = wbwd.at[offsets[h], wrow(k), here]
+            arrived(ref, br.at[i, h])
+            if i == h:
+                copy = remote(ref, ref, bs2.at[i], br2.at[i], at(z, x + to), s)
+                copy.start()
+                waits.append(copy)
+            w_along_y(i, k, h)
+
+    @pl.when(zmine)
+    def _():
+        own_forward().wait()
+
     for k in range(1, NZC):
         source = lax.rem(z - k + NZC, NZC)
-        arrived(wrecv.at[:, source, x], wr.at[k - 1])
-    for i, k in enumerate((1, -1)):
-        ref = wrecv.at[:, :, x]
-        copy = remote(ref, ref, fs.at[i], fr.at[i], at(z, x + k), s)
-        copy.start()
-        waits.append(copy)
+
+        @pl.when(lax.rem(source, 2) == par)
+        def _():
+            arrived(wrecv.at[:, source // 2, par, x], wr.at[k - 1])
+
+    for h in range(2):
+        for i, k in enumerate((1, -1)):
+            ref = wrecv.at[:, pairs[h], par, x]
+            copy = remote(ref, ref, fs.at[i, h], fr.at[i, h], at(z, x + k), s)
+            copy.start()
+            waits.append(copy)
+        f_along_y(2, 0, h)
+
+    hop(1)
+
+    for h in range(2):
+        arrived(wbwd.at[offsets[h], wrow(2), here], br2.at[h])
+        w_along_y(2, 2, h)
+    for h in range(2):
+        for i, (k, to) in enumerate(((-1, 1), (1, -1))):
+            ref = wrecv.at[:, pairs[h], par, lax.rem(x + k + NXC, NXC)]
+            arrived(ref, fr.at[i, h])
+            if i == h:
+                copy = remote(ref, ref, fs2.at[i], fr2.at[i], at(z, x + to), s)
+                copy.start()
+                waits.append(copy)
+            f_along_y(i, k, h)
 
     hop(2)
 
-    for i, (k, to) in enumerate(((-1, 1), (1, -1))):
-        source = lax.rem(x + k + NXC, NXC)
-        arrived(wrecv.at[:, :, source], fr.at[i])
-        ref = wrecv.at[:, pl.ds(4 * i, 4), source]
-        copy = remote(ref, ref, fs.at[2 + i], fr.at[2 + i], at(z, x + to), s)
-        copy.start()
-        waits.append(copy)
-    for i, lanes in enumerate((low, high)):
-        arrived(wbwd.at[:, wrow(2), lanes], br.at[2 + i])
+    for h in range(2):
+        arrived(wrecv.at[:, pairs[h], par, lax.rem(x + 2, NXC)], fr2.at[h])
+        f_along_y(3, 2, h)
+    for h in range(2):
+        for j, k in enumerate((-1, 1, 2)):
+            arrived(wbwd.at[offsets[h], wrow(k), there], ybr.at[j, h])
     theirs = pl.ds(pl.multiple_of(sib * 32, 32), 32)
     mine = pl.ds(pl.multiple_of(s * 32, 32), 32)
     swap = remote(
@@ -237,6 +319,23 @@
 
     lane_z = iota((32, 128), 1) % 16
     lane_k = iota((512, 128), 1) % 8
+
+    def send_out(t, to):
+        for j in range(2):
+            owner = 2 * s + j
+            src = outs.at[t, j, pl.ds(4 * to, 4)]
+            dst = outr.at[t, x]
+            itself = jnp.logical_and(owner == x, s == to)
+
+            @pl.when(itself)
+            def _():
+                pltpu.make_async_copy(src, dst, or_.at[t, x]).start()
+
+            @pl.when(jnp.logical_not(itself))
+            def _():
+                remote(
+                    src, dst, os_.at[t, j, to], or_.at[t, x], at(z, owner), to
+                ).start()
 
     def conv(weights_of, t):
         sign = 1 if t == 0 else -1
@@ -289,32 +388,18 @@
                 result = result.astype(BF)
                 for j in range(2):
                     outs[t, j, plane] = result[16 * j : 16 * j + 16]
-
-        for j in range(2):
-            for to in range(2):
-                owner = 2 * s + j
-                src = outs.at[t, j, pl.ds(4 * to, 4)]
-                dst = outr.at[t, x]
-                itself = jnp.logical_and(owner == x, s == to)
-
-                @pl.when(itself)
-                def _():
-                    pltpu.make_async_copy(src, dst, or_.at[t, x]).start()
-
-                @pl.when(jnp.logical_not(itself))
-                def _():
-                    remote(
-                        src, dst, os_.at[t, j, to], or_.at[t, x], at(z, owner), to
-                    ).start()
+            if pair % 2:
+                send_out(t, pair // 2)
 
     def bwd_rows(ai):
         return wbwd[9 * ai : 9 * ai + 9, mine, :].reshape(288, 512)
 
     conv(bwd_rows, 0)
 
-    for i in range(2):
-        source = lax.rem(x + 2, NXC)
-        arrived(wrecv.at[:, pl.ds(4 * i, 4), source], fr.at[2 + i])
+    for h in range(2):
+        for j, k in enumerate((-1, 1, 0, 2)):
+            column = lax.rem(x + k + NXC, NXC)
+            arrived(wrecv.at[:, pairs[h], 1 - par, column], yfr.at[j, h])
     for g in range(7):
         wfwd[128 * g : 128 * g + 128, :] = wrecv[g].reshape(512, 128).T
 
@@ -332,6 +417,12 @@
 
     for copy in waits:
         copy.wait_send()
+
+    @pl.when(zmine)
+    def _():
+        for k in range(1, NZC):
+            to_z(k).wait_send()
+
     for t in range(2):
         for j in range(2):
             for to in range(2):
@@ -348,25 +439,26 @@
 def per_device(inputs, weights, out_grad):
     chans, slab_len, plane_size = inputs.shape
 
-    def rows(block):
-        return block.transpose(1, 0, 2).reshape(slab_len * chans, plane_size)
-
     vmem = pl.BlockSpec(memory_space=pltpu.VMEM)
     shape = jax.ShapeDtypeStruct((slab_len * chans, plane_size), BF)
     dma = pltpu.SemaphoreType.DMA
     grad, conv = pl.pallas_call(
         kernel,
         out_shape=(shape, shape),
-        in_specs=[vmem] * 3,
+        in_specs=[pl.BlockSpec(memory_space=pl.ANY)] * 3,
         out_specs=(vmem, vmem),
         scratch_shapes=[
+            pltpu.VMEM((2, 16, 4, 512), BF),
+            pltpu.VMEM((8, 64, 128), F32),
+            pltpu.VMEM((27, 16, 512), BF),
+            dma((3,)),
             pltpu.VMEM((512, 1024), BF),
             pltpu.VMEM((512, 256), BF),
             pltpu.VMEM((4, 9, 16, 128), BF),
             pltpu.VMEM((2, 9, 512, 128), BF),
             pltpu.VMEM((4, 112, 512), BF),
             pltpu.VMEM((8, 7, 16, 128), BF),
-            pltpu.VMEM((7, 8, 4, 16, 128), BF),
+            pltpu.VMEM((7, 4, 2, 4, 16, 128), BF),
             pltpu.VMEM((896, 512), BF),
             pltpu.VMEM((27, 64, 512), BF),
             pltpu.VMEM((2, 2, 8, 16, 128), BF),
@@ -374,18 +466,18 @@
             pltpu.VMEM((3, 288, 128), F32),
             dma((3,)),
             dma((3, 2)), dma((3, 2)),
-            dma((2, 4, 2)), dma((2, 4, 2)),
+            dma((2, 4, 4)), dma((2, 4, 4)),
             dma((8, 2)), dma((8, 2)),
             dma((7,)), dma((7,)),
-            dma((4,)), dma((4,)),
-            dma((4,)), dma((4,)),
+            dma((2, 2)), dma((2, 2)), dma((2,)), dma((2,)), dma((4, 2)), dma((4, 2)),
+            dma((2, 2)), dma((2, 2)), dma((2,)), dma((2,)), dma((3, 2)), dma((3, 2)),
             dma((1,)), dma((1,)),
             dma((2, 2, 2)), dma((2, 4)),
         ],
         compiler_params=pltpu.CompilerParams(
-            collective_id=0, has_side_effects=True, vmem_limit_bytes=48 * 1024 * 1024
+            collective_id=0, has_side_effects=True, vmem_limit_bytes=60 * 1024 * 1024
         ),
-    )(rows(out_grad), rows(inputs), weights)
+    )(out_grad, inputs, weights)
 
     def back(block):
         return block.reshape(slab_len, chans, plane_size).transpose(1, 0, 2)

time: 44.7 us -> 42 us (0.940)
  Pallas kernels: 41.2 us -> 39.6 us
  local copies, waits for them, and re-layouts: 2.67 us -> 1.63 us
    pallas_call x1, Pallas kernels: 41.2 us -> 39.6 us  [per_device(): pl.pallas_call(kernel, out_shape=(shape, shape), in_specs=[pl.BlockSpec(m...]
    unnamed x4 -> x0, local copies, waits for them, and re-layouts: 1.01 us -> none
    transpose x2 -> x0, local copies, waits for them, and re-layouts: 0.9 us -> none  [rows(): return block.transpose(1, 0, 2).reshape(slab_len * chans, plane_size)]
    transpose x1, local copies, waits for them, and re-layouts: 0.75 us -> 1.63 us  [back(): return block.reshape(slab_len, chans, plane_size).transpose(1, 0, 2)]
where the time goes in v2:
time: 42 us; the launch traced here: 41.8 us
  Pallas kernels  39.6 us (94%)
  local copies, waits for them, and re-layouts  1.63 us (4%)
  between operations  0.64 us (2%)
    pallas_call x1, Pallas kernels, per_device(): pl.pallas_call(kernel, out_shape=(shape, shape), in_specs=[pl.BlockSpec(m...  39.6 us
    transpose x1, local copies, waits for them, and re-layouts, back(): return block.reshape(slab_len, chans, plane_size).transpose(1, 0, 2)  1.63 us

profile of v2, /device:TPU:1, one launch (start us, length us, event | category | flops | bytes accessed | tf_op | source)
XLA Modules:
  0.0 41.8 jit_solution(6615325448474180055)
XLA Ops:
  0.6 39.6 %shard_map.50 = (bf16[64,512]{1,0:T(8,128)(2,1)}, bf16[64,512]{1,0:T(8,128)(2,1)}) custom-call(bf16[16,4,512]{2,1,0:T(4,128)(2,1)} %g_hbm.1, bf16[16,4,512]{2,1,0:T(4,128)(2,1)} %x_hbm.1, bf16[27,16,512]{2,1,0:T(8,128)(2,1)} %w_hbm.1), custom_call_target="tpu_custom_call" | custom-call | tf_op jit(solution)/shard_map/pallas_call | solution.py:445
  40.2 1.6 %copy_bitcast_fusion = (bf16[16,4,512]{2,1,0:T(4,128)(2,1)}, bf16[16,4,512]{2,1,0:T(4,128)(2,1)}) fusion(bf16[4,16,512]{2,1,0:T(8,128)(2,1)} %bitcast.6, bf16[4,16,512]{2,1,0:T(8,128)(2,1)} %bitcast.7), kind=kLoop, calls=%fused_computation | loop fusion | bytes 262144 | tf_op jit(solution)/shard_map/transpose | solution.py:483

commit v3 on v2

--- a/solution.py
+++ b/solution.py
@@ -39,8 +39,8 @@
     g_hbm, x_hbm, w_hbm, go_ref, co_ref,
     raw, tall, w_ref, in_sem,
     perm, permw, part, acts, wl, wpack, wrecv, wfwd, wbwd, outs, outr, hprod,
-    loc_sem, xs, xr, zs, zr, ss, sr, ws, wr, fs, fr, fs2, fr2, yfs, yfr,
-    bs, br, bs2, br2, ybs, ybr, bx, by, os_, or_,
+    loc_sem, xs, xr, zs, zr, ss, sr, ws, wr, fs, fr, yfs, yfr,
+    bs, br, ybs, ybr, bx, by, os_, or_,
 ):
     fetch = [
         pltpu.make_async_copy(src, dst, in_sem.at[i])
@@ -146,18 +146,17 @@
         w_ref.at[:, :, half], wbwd.at[:, wrow(0), half], loc_sem.at[1]
     )
     own_w.start()
-    for h in range(2):
-        for i, k in enumerate((1, -1)):
-            copy = remote(
-                w_ref.at[offsets[h], :, here], wbwd.at[offsets[h], wrow(0), here],
-                bs.at[i, h], br.at[i, h], at(z, x + k), s,
-            )
-            copy.start()
-            waits.append(copy)
-
-    def w_along_y(j, k, h):
-        ref = wbwd.at[offsets[h], wrow(k), here]
-        copy = remote(ref, ref, ybs.at[j, h], ybr.at[j, h], chan, s, y_next[h])
+    for k in (1, 3, 2):
+        copy = remote(
+            w_ref.at[:, :, here], wbwd.at[:, wrow(0), here],
+            bs.at[k - 1], br.at[k - 1], at(z, x + k), s,
+        )
+        copy.start()
+        waits.append(copy)
+
+    def w_along_y(k, h):
+        ref = wbwd.at[offsets[h], wrow(-k), here]
+        copy = remote(ref, ref, ybs.at[k - 1, h], ybr.at[k - 1, h], chan, s, y_next[h])
         copy.start()
         waits.append(copy)
 
@@ -198,9 +197,9 @@
 
     pairs = (pl.ds(0, 2), pl.ds(2, 2))
 
-    def f_along_y(j, k, h):
-        ref = wrecv.at[:, pairs[h], par, lax.rem(x + k + NXC, NXC)]
-        copy = remote(ref, ref, yfs.at[j, h], yfr.at[j, h], chan, s, y_next[h])
+    def f_along_y(k, h):
+        ref = wrecv.at[:, pairs[h], par, lax.rem(x - k + NXC, NXC)]
+        copy = remote(ref, ref, yfs.at[k, h], yfr.at[k, h], chan, s, y_next[h])
         copy.start()
         waits.append(copy)
 
@@ -238,84 +237,78 @@
     def hop(h):
         for c in range(4):
             for direction in range(2):
-                if h == 4 and c // 2 != direction:
+                if h == 4 and c % 2 != direction:
                     continue
                 k = -h if direction == 0 else h
                 arrived(acts.at[s, chunk[c], block(k)], zr.at[direction, h - 1, c])
-                if h < 3 or (h == 3 and c // 2 == direction):
+                if h < 3 or (h == 3 and c % 2 == direction):
                     pass_on(k, c, direction, h)
                 if c % 2:
-                    to_sibling(k, c // 2)
-
-    own_w.wait()
-    for h in range(2):
-        for i, (k, to) in enumerate(((-1, 1), (1, -1))):
-            ref = wbwd.at[offsets[h], wrow(k), here]
-            arrived(ref, br.at[i, h])
-            if i == h:
-                copy = remote(ref, ref, bs2.at[i], br2.at[i], at(z, x + to), s)
-                copy.start()
-                waits.append(copy)
-            w_along_y(i, k, h)
-
-    @pl.when(zmine)
-    def _():
-        own_forward().wait()
-
-    for k in range(1, NZC):
-        source = lax.rem(z - k + NZC, NZC)
-
-        @pl.when(lax.rem(source, 2) == par)
+                    to_sibling(4 if h == 4 else k, c // 2)
+
+    theirs = pl.ds(pl.multiple_of(sib * 32, 32), 32)
+    mine = pl.ds(pl.multiple_of(s * 32, 32), 32)
+
+    def back_x():
+        own_w.wait()
+        for k in (1, 3, 2):
+            arrived(wbwd.at[:, wrow(-k), here], br.at[k - 1])
+            for h in range(2):
+                w_along_y(k, h)
+
+    def forward_z():
+        @pl.when(zmine)
         def _():
-            arrived(wrecv.at[:, source // 2, par, x], wr.at[k - 1])
-
-    for h in range(2):
-        for i, k in enumerate((1, -1)):
-            ref = wrecv.at[:, pairs[h], par, x]
-            copy = remote(ref, ref, fs.at[i, h], fr.at[i, h], at(z, x + k), s)
+            own_forward().wait()
+
+        for k in range(1, NZC):
+            source = lax.rem(z - k + NZC, NZC)
+
+            @pl.when(lax.rem(source, 2) == par)
+            def _():
+                arrived(wrecv.at[:, source // 2, par, x], wr.at[k - 1])
+
+        for k in (1, 3, 2):
+            ref = wrecv.at[:, :, par, x]
+            copy = remote(ref, ref, fs.at[k - 1], fr.at[k - 1], at(z, x + k), s)
             copy.start()
             waits.append(copy)
-        f_along_y(2, 0, h)
-
+        for h in range(2):
+            f_along_y(0, h)
+
+    def forward_x():
+        for k in (1, 3, 2):
+            arrived(wrecv.at[:, :, par, lax.rem(x - k + NXC, NXC)], fr.at[k - 1])
+            for h in range(2):
+                f_along_y(k, h)
+
+    def back_y():
+        for h in range(2):
+            for k in (1, 3, 2):
+                arrived(wbwd.at[offsets[h], wrow(-k), there], ybr.at[k - 1, h])
+        swap = remote(
+            wbwd.at[:, theirs, half], wbwd.at[:, theirs, half], bx.at[0], by.at[0], at(z, x), sib
+        )
+        swap.start()
+        waits.append(swap)
+
+    back_x()
     hop(1)
-
-    for h in range(2):
-        arrived(wbwd.at[offsets[h], wrow(2), here], br2.at[h])
-        w_along_y(2, 2, h)
-    for h in range(2):
-        for i, (k, to) in enumerate(((-1, 1), (1, -1))):
-            ref = wrecv.at[:, pairs[h], par, lax.rem(x + k + NXC, NXC)]
-            arrived(ref, fr.at[i, h])
-            if i == h:
-                copy = remote(ref, ref, fs2.at[i], fr2.at[i], at(z, x + to), s)
-                copy.start()
-                waits.append(copy)
-            f_along_y(i, k, h)
-
+    forward_z()
     hop(2)
-
-    for h in range(2):
-        arrived(wrecv.at[:, pairs[h], par, lax.rem(x + 2, NXC)], fr2.at[h])
-        f_along_y(3, 2, h)
-    for h in range(2):
-        for j, k in enumerate((-1, 1, 2)):
-            arrived(wbwd.at[offsets[h], wrow(k), there], ybr.at[j, h])
-    theirs = pl.ds(pl.multiple_of(sib * 32, 32), 32)
-    mine = pl.ds(pl.multiple_of(s * 32, 32), 32)
-    swap = remote(
-        wbwd.at[:, theirs, half], wbwd.at[:, theirs, half], bx.at[0], by.at[0], at(z, x), sib
-    )
-    swap.start()
-    waits.append(swap)
-
+    forward_x()
     hop(3)
+    back_y()
     hop(4)
 
     other = pl.ds(pl.multiple_of(sib * 256, 128), 256)
     arrived(wbwd.at[:, mine, other], by.at[0])
-    for i in range(2):
+
+    def from_sibling(i):
         for k in range(NZC):
             arrived(acts.at[sib, span[i], block(k)], sr.at[k, i])
+
+    from_sibling(0)
 
     lane_z = iota((32, 128), 1) % 16
     lane_k = iota((512, 128), 1) % 8
@@ -337,12 +330,12 @@
                     src, dst, os_.at[t, j, to], or_.at[t, x], at(z, owner), to
                 ).start()
 
-    def conv(weights_of, t):
+    def conv_of(weights_of, t):
         sign = 1 if t == 0 else -1
         first, second = (0, 1) if t == 0 else (1, 0)
         edge = jnp.where(lane_k < 4, acts[first, 4], acts[second, 4])
         for ai in range(3):
-            hprod[ai] = jnp.dot(weights_of(ai), edge, preferred_element_type=F32)
+            hprod[3 * t + ai] = jnp.dot(weights_of(ai), edge, preferred_element_type=F32)
 
         def over_y(read, ci):
             total = read(3 + ci)
@@ -354,56 +347,64 @@
         edges = {}
         for ai in range(3):
             for ci in (0, 2):
-                edges[ai, ci] = over_y(lambda r: hprod[ai, 32 * r : 32 * r + 32], ci)
-        for pair in range(4):
-            total = None
-            for ai in range(3):
-                planes = [(2 * pair + i - sign * (ai - 1)) % 8 for i in range(2)]
-                both = jnp.concatenate(
-                    [acts[p // 4, 5 * t + p % 4] for p in planes], axis=1
-                )
-                term = jnp.dot(weights_of(ai), both, preferred_element_type=F32)
-                total = term if total is None else total + term
-            for i in range(2):
-                plane = 2 * pair + i
-                cells = total[:, 128 * i : 128 * i + 128]
-
-                def read(r):
-                    return cells[32 * r : 32 * r + 32]
-
-                result = over_y(read, 1)
-                for ci in (0, 2):
-                    e = sign * (ci - 1)
-                    moved = pltpu.roll(over_y(read, ci), e % 128, 1)
-                    outside = None
-                    for ai in range(3):
-                        source = (plane - sign * (ai - 1) + 4 * t) % 8
-                        shift = (-source if e == 1 else 7 - source) % 128
-                        term = edges[ai, ci]
-                        if shift:
-                            term = pltpu.roll(term, shift, 1)
-                        outside = term if outside is None else outside + term
-                    border = lane_z == (0 if e == 1 else 15)
-                    result = result + jnp.where(border, outside, moved)
-                result = result.astype(BF)
-                for j in range(2):
-                    outs[t, j, plane] = result[16 * j : 16 * j + 16]
-            if pair % 2:
-                send_out(t, pair // 2)
+                edges[ai, ci] = over_y(lambda r: hprod[3 * t + ai, 32 * r : 32 * r + 32], ci)
+        def planes_of(to):
+            for pair in (2 * to, 2 * to + 1):
+                total = None
+                for ai in range(3):
+                    planes = [(2 * pair + i - sign * (ai - 1)) % 8 for i in range(2)]
+                    both = jnp.concatenate(
+                        [acts[p // 4, 5 * t + p % 4] for p in planes], axis=1
+                    )
+                    term = jnp.dot(weights_of(ai), both, preferred_element_type=F32)
+                    total = term if total is None else total + term
+                for i in range(2):
+                    plane = 2 * pair + i
+                    cells = total[:, 128 * i : 128 * i + 128]
+
+                    def read(r):
+                        return cells[32 * r : 32 * r + 32]
+
+                    result = over_y(read, 1)
+                    for ci in (0, 2):
+                        e = sign * (ci - 1)
+                        moved = pltpu.roll(over_y(read, ci), e % 128, 1)
+                        outside = None
+                        for ai in range(3):
+                            source = (plane - sign * (ai - 1) + 4 * t) % 8
+                            shift = (-source if e == 1 else 7 - source) % 128
+                            term = edges[ai, ci]
+                            if shift:
+                                term = pltpu.roll(term, shift, 1)
+                            outside = term if outside is None else outside + term
+                        border = lane_z == (0 if e == 1 else 15)
+                        result = result + jnp.where(border, outside, moved)
+                    result = result.astype(BF)
+                    for j in range(2):
+                        outs[t, j, plane] = result[16 * j : 16 * j + 16]
+            send_out(t, to)
+
+        return planes_of
 
     def bwd_rows(ai):
         return wbwd[9 * ai : 9 * ai + 9, mine, :].reshape(288, 512)
 
-    conv(bwd_rows, 0)
+    back = conv_of(bwd_rows, 0)
+    back(1)
+
+    from_sibling(1)
 
     for h in range(2):
-        for j, k in enumerate((-1, 1, 0, 2)):
-            column = lax.rem(x + k + NXC, NXC)
-            arrived(wrecv.at[:, pairs[h], 1 - par, column], yfr.at[j, h])
+        for k in (0, 1, 3, 2):
+            column = lax.rem(x - k + NXC, NXC)
+            arrived(wrecv.at[:, pairs[h], 1 - par, column], yfr.at[k, h])
     for g in range(7):
         wfwd[128 * g : 128 * g + 128, :] = wrecv[g].reshape(512, 128).T
 
-    conv(lambda ai: wfwd[288 * ai : 288 * ai + 288, :], 1)
+    forth = conv_of(lambda ai: wfwd[288 * ai : 288 * ai + 288, :], 1)
+    forth(1)
+    back(0)
+    forth(0)
 
     for t, ref in ((0, go_ref), (1, co_ref)):
         for q in range(NXC):
@@ -463,14 +464,14 @@
             pltpu.VMEM((27, 64, 512), BF),
             pltpu.VMEM((2, 2, 8, 16, 128), BF),
             pltpu.VMEM((2, 4, 4, 16, 128), BF),
-            pltpu.VMEM((3, 288, 128), F32),
+            pltpu.VMEM((6, 288, 128), F32),
             dma((3,)),
             dma((3, 2)), dma((3, 2)),
             dma((2, 4, 4)), dma((2, 4, 4)),
             dma((8, 2)), dma((8, 2)),
             dma((7,)), dma((7,)),
-            dma((2, 2)), dma((2, 2)), dma((2,)), dma((2,)), dma((4, 2)), dma((4, 2)),
-            dma((2, 2)), dma((2, 2)), dma((2,)), dma((2,)), dma((3, 2)), dma((3, 2)),
+            dma((3,)), dma((3,)), dma((4, 2)), dma((4, 2)),
+            dma((3,)), dma((3,)), dma((3, 2)), dma((3, 2)),
             dma((1,)), dma((1,)),
             dma((2, 2, 2)), dma((2, 4)),
         ],

time: 42 us -> 41.3 us (0.983)
  the two profiles are of different devices: /device:TPU:1 before, /device:TPU:16 now
where the time goes in v3:
time: 41.3 us; the launch traced here: 41.2 us
  Pallas kernels  38.9 us (94%)
  local copies, waits for them, and re-layouts  1.63 us (4%)
  between operations  0.64 us (2%)
    pallas_call x1, Pallas kernels, per_device(): pl.pallas_call(kernel, out_shape=(shape, shape), in_specs=[pl.BlockSpec(m...  38.9 us
    transpose x1, local copies, waits for them, and re-layouts, back(): return block.reshape(slab_len, chans, plane_size).transpose(1, 0, 2)  1.63 us

profile of v3, /device:TPU:16, one launch (start us, length us, event | category | flops | bytes accessed | tf_op | source)
XLA Modules:
  0.0 41.2 jit_solution(10538578845357258898)
XLA Ops:
  0.6 38.9 %shard_map.50 = (bf16[64,512]{1,0:T(8,128)(2,1)}, bf16[64,512]{1,0:T(8,128)(2,1)}) custom-call(bf16[16,4,512]{2,1,0:T(4,128)(2,1)} %g_hbm.1, bf16[16,4,512]{2,1,0:T(4,128)(2,1)} %x_hbm.1, bf16[27,16,512]{2,1,0:T(8,128)(2,1)} %w_hbm.1), custom_call_target="tpu_custom_call" | custom-call | tf_op jit(solution)/shard_map/pallas_call | solution.py:446
  39.6 1.6 %copy_bitcast_fusion = (bf16[16,4,512]{2,1,0:T(4,128)(2,1)}, bf16[16,4,512]{2,1,0:T(4,128)(2,1)}) fusion(bf16[4,16,512]{2,1,0:T(8,128)(2,1)} %bitcast.6, bf16[4,16,512]{2,1,0:T(8,128)(2,1)} %bitcast.7), kind=kLoop, calls=%fused_computation | loop fusion | bytes 262144 | tf_op jit(solution)/shard_map/transpose | solution.py:484

commit v4 on v3

--- a/solution.py
+++ b/solution.py
@@ -476,7 +476,7 @@
             dma((2, 2, 2)), dma((2, 4)),
         ],
         compiler_params=pltpu.CompilerParams(
-            collective_id=0, has_side_effects=True, vmem_limit_bytes=60 * 1024 * 1024
+            collective_id=0, has_side_effects=True, vmem_limit_bytes=55104 * 1024
         ),
     )(out_grad, inputs, weights)
 

time: 41.3 us -> 39.8 us (0.964)
  local copies, waits for them, and re-layouts: 1.63 us -> 0.75 us
  Pallas kernels: 38.9 us -> 38.3 us
    transpose x1, local copies, waits for them, and re-layouts: 1.63 us -> 0.75 us  [back(): return block.reshape(slab_len, chans, plane_size).transpose(1, 0, 2)]
    pallas_call x1, Pallas kernels: 38.9 us -> 38.3 us  [per_device(): pl.pallas_call(kernel, out_shape=(shape, shape), in_specs=[pl.BlockSpec(m...]
where the time goes in v4:
time: 39.8 us; the launch traced here: 39.7 us
  Pallas kernels  38.3 us (96%)
  local copies, waits for them, and re-layouts  0.75 us (2%)
  between operations  0.64 us (2%)
    pallas_call x1, Pallas kernels, per_device(): pl.pallas_call(kernel, out_shape=(shape, shape), in_specs=[pl.BlockSpec(m...  38.3 us

profile of v4, /device:TPU:16, one launch (start us, length us, event | category | flops | bytes accessed | tf_op | source)
XLA Modules:
  0.0 39.7 jit_solution(9024961942178966623)
XLA Ops:
  0.6 38.3 %shard_map.50 = (bf16[64,512]{1,0:T(8,128)(2,1)S(1)}, bf16[64,512]{1,0:T(8,128)(2,1)S(1)}) custom-call(bf16[16,4,512]{2,1,0:T(4,128)(2,1)} %g_hbm.1, bf16[16,4,512]{2,1,0:T(4,128)(2,1)} %x_hbm.1, bf16[27,16,512]{2,1,0:T(8,128)(2,1)} %w_hbm.1), custom_call_target="tpu_custom_call" | custom-call | tf_op jit(solution)/shard_map/pallas_call | solution.py:446
  38.9 0.8 %copy_bitcast_fusion = (bf16[16,4,512]{2,1,0:T(4,128)(2,1)}, bf16[16,4,512]{2,1,0:T(4,128)(2,1)}) fusion(bf16[4,16,512]{2,1,0:T(8,128)(2,1)S(1)} %bitcast.6, bf16[4,16,512]{2,1,0:T(8,128)(2,1)S(1)} %bitcast.7), kind=kLoop, calls=%fused_computation | loop fusion | bytes 262144 | tf_op jit(solution)/shard_map/transpose | solution.py:484

commit v5 on v4

--- a/solution.py
+++ b/solution.py
@@ -119,7 +119,7 @@
 
     my_rows = pl.ds(pl.multiple_of(chan * 16, 16), 16)
     span = (pl.ds(0, 5), pl.ds(5, 4))
-    chunk = (pl.ds(0, 2), pl.ds(2, 3), pl.ds(5, 2), pl.ds(7, 2))
+    chunk = (pl.ds(0, 3), pl.ds(3, 2), pl.ds(5, 2), pl.ds(7, 2))
     waits = []
     own = pltpu.make_async_copy(part.at[x], acts.at[s, :, my_rows], loc_sem.at[0])
     own.start()
@@ -297,8 +297,8 @@
     forward_z()
     hop(2)
     forward_x()
+    back_y()
     hop(3)
-    back_y()
     hop(4)
 
     other = pl.ds(pl.multiple_of(sib * 256, 128), 256)
@@ -406,6 +406,14 @@
     back(0)
     forth(0)
 
+    for copy in waits:
+        copy.wait_send()
+
+    @pl.when(zmine)
+    def _():
+        for k in range(1, NZC):
+            to_z(k).wait_send()
+
     for t, ref in ((0, go_ref), (1, co_ref)):
         for q in range(NXC):
             arrived(outr.at[t, q], or_.at[t, q])
@@ -415,14 +423,6 @@
         ref[...] = lax.dot_general(
             joined, perm[:, 0:512], (((1,), (1,)), ((), ())), preferred_element_type=F32
         ).astype(BF)
-
-    for copy in waits:
-        copy.wait_send()
-
-    @pl.when(zmine)
-    def _():
-        for k in range(1, NZC):
-            to_z(k).wait_send()
 
     for t in range(2):
         for j in range(2):

time: 39.8 us -> 39.4 us (0.990)
  Pallas kernels: 38.3 us -> 37.9 us
    pallas_call x1, Pallas kernels: 38.3 us -> 37.9 us  [per_device(): pl.pallas_call(kernel, out_shape=(shape, shape), in_specs=[pl.BlockSpec(m...]
where the time goes in v5:
time: 39.4 us; the launch traced here: 39.3 us
  Pallas kernels  37.9 us (96%)
  local copies, waits for them, and re-layouts  0.75 us (2%)
  between operations  0.64 us (2%)
    pallas_call x1, Pallas kernels, per_device(): pl.pallas_call(kernel, out_shape=(shape, shape), in_specs=[pl.BlockSpec(m...  37.9 us

profile of v5, /device:TPU:16, one launch (start us, length us, event | category | flops | bytes accessed | tf_op | source)
XLA Modules:
  0.0 39.3 jit_solution(3935341562956921888)
XLA Ops:
  0.6 37.9 %shard_map.50 = (bf16[64,512]{1,0:T(8,128)(2,1)S(1)}, bf16[64,512]{1,0:T(8,128)(2,1)S(1)}) custom-call(bf16[16,4,512]{2,1,0:T(4,128)(2,1)} %g_hbm.1, bf16[16,4,512]{2,1,0:T(4,128)(2,1)} %x_hbm.1, bf16[27,16,512]{2,1,0:T(8,128)(2,1)} %w_hbm.1), custom_call_target="tpu_custom_call" | custom-call | tf_op jit(solution)/shard_map/pallas_call | solution.py:446
  38.5 0.8 %copy_bitcast_fusion = (bf16[16,4,512]{2,1,0:T(4,128)(2,1)}, bf16[16,4,512]{2,1,0:T(4,128)(2,1)}) fusion(bf16[4,16,512]{2,1,0:T(8,128)(2,1)S(1)} %bitcast.6, bf16[4,16,512]{2,1,0:T(8,128)(2,1)S(1)} %bitcast.7), kind=kLoop, calls=%fused_computation | loop fusion | bytes 262144 | tf_op jit(solution)/shard_map/transpose | solution.py:484

commit v6 on v5

--- a/solution.py
+++ b/solution.py
@@ -123,15 +123,14 @@
     waits = []
     own = pltpu.make_async_copy(part.at[x], acts.at[s, :, my_rows], loc_sem.at[0])
     own.start()
-    for i in range(2):
-        for k in (1, 3, 2):
-            dest = lax.rem(x + k, NXC)
-            copy = remote(
-                part.at[dest, span[i]], acts.at[s, span[i], my_rows],
-                xs.at[k - 1, i], xr.at[k - 1, i], at(z, dest), s,
-            )
-            copy.start()
-            waits.append(copy)
+    for k in (2, 1, 3):
+        dest = lax.rem(x + k, NXC)
+        copy = remote(
+            part.at[dest], acts.at[s, :, my_rows],
+            xs.at[k - 1, 0], xr.at[k - 1, 0], at(z, dest), s,
+        )
+        copy.start()
+        waits.append(copy)
 
     half = pl.ds(pl.multiple_of(s * 256, 128), 256)
     here = pl.ds(pl.multiple_of(s * 256 + par * 128, 128), 128)
@@ -224,11 +223,10 @@
         waits.append(copy)
 
     own.wait()
+    for k in (1, 3, 2):
+        rows = pl.ds(pl.multiple_of(at(z, x - k) * 16, 16), 16)
+        arrived(acts.at[s, :, rows], xr.at[k - 1, 0])
     for i in range(2):
-        for k in (1, 3, 2):
-            source = lax.rem(x - k + NXC, NXC)
-            rows = pl.ds(pl.multiple_of((z * NXC + source) * 16, 16), 16)
-            arrived(acts.at[s, span[i], rows], xr.at[k - 1, i])
         for c in (2 * i, 2 * i + 1):
             pass_on(0, c, 0, 0)
             pass_on(0, c, 1, 0)

time: 39.4 us -> 39.4 us (level)
  no operation moved by 1% of the time
where the time goes in v6:
time: 39.4 us; the launch traced here: 39.3 us
  Pallas kernels  37.9 us (96%)
  local copies, waits for them, and re-layouts  0.75 us (2%)
  between operations  0.64 us (2%)
    pallas_call x1, Pallas kernels, per_device(): pl.pallas_call(kernel, out_shape=(shape, shape), in_specs=[pl.BlockSpec(m...  37.9 us

profile of v6, /device:TPU:16, one launch (start us, length us, event | category | flops | bytes accessed | tf_op | source)
XLA Modules:
  0.0 39.3 jit_solution(11723442114486536163)
XLA Ops:
  0.6 37.9 %shard_map.50 = (bf16[64,512]{1,0:T(8,128)(2,1)S(1)}, bf16[64,512]{1,0:T(8,128)(2,1)S(1)}) custom-call(bf16[16,4,512]{2,1,0:T(4,128)(2,1)} %g_hbm.1, bf16[16,4,512]{2,1,0:T(4,128)(2,1)} %x_hbm.1, bf16[27,16,512]{2,1,0:T(8,128)(2,1)} %w_hbm.1), custom_call_target="tpu_custom_call" | custom-call | tf_op jit(solution)/shard_map/pallas_call | solution.py:444
  38.5 0.8 %copy_bitcast_fusion = (bf16[16,4,512]{2,1,0:T(4,128)(2,1)}, bf16[16,4,512]{2,1,0:T(4,128)(2,1)}) fusion(bf16[4,16,512]{2,1,0:T(8,128)(2,1)S(1)} %bitcast.6, bf16[4,16,512]{2,1,0:T(8,128)(2,1)S(1)} %bitcast.7), kind=kLoop, calls=%fused_computation | loop fusion | bytes 262144 | tf_op jit(solution)/shard_map/transpose | solution.py:482

commit v7 on v6

--- a/solution.py
+++ b/solution.py
@@ -305,6 +305,13 @@
     def from_sibling(i):
         for k in range(NZC):
             arrived(acts.at[sib, span[i], block(k)], sr.at[k, i])
+
+    for h in range(2):
+        for k in (0, 1, 3, 2):
+            column = lax.rem(x - k + NXC, NXC)
+            arrived(wrecv.at[:, pairs[h], 1 - par, column], yfr.at[k, h])
+    for g in range(7):
+        wfwd[128 * g : 128 * g + 128, :] = wrecv[g].reshape(512, 128).T
 
     from_sibling(0)
 
@@ -391,13 +398,6 @@
     back(1)
 
     from_sibling(1)
-
-    for h in range(2):
-        for k in (0, 1, 3, 2):
-            column = lax.rem(x - k + NXC, NXC)
-            arrived(wrecv.at[:, pairs[h], 1 - par, column], yfr.at[k, h])
-    for g in range(7):
-        wfwd[128 * g : 128 * g + 128, :] = wrecv[g].reshape(512, 128).T
 
     forth = conv_of(lambda ai: wfwd[288 * ai : 288 * ai + 288, :], 1)
     forth(1)

time: 39.4 us -> 40.2 us (1.020); the launches traced: 39.3 us -> 39.5 us
  no operation moved by 1% of the time
where the time goes in v7:
time: 40.2 us; the launch traced here: 39.5 us
  Pallas kernels  38.1 us (95%)
  local copies, waits for them, and re-layouts  0.75 us (2%)
  between operations  0.64 us (2%)
    pallas_call x1, Pallas kernels, per_device(): pl.pallas_call(kernel, out_shape=(shape, shape), in_specs=[pl.BlockSpec(m...  38.1 us

profile of v7, /device:TPU:16, one launch (start us, length us, event | category | flops | bytes accessed | tf_op | source)
XLA Modules:
  0.0 39.5 jit_solution(11747128683957467773)
XLA Ops:
  0.6 38.1 %shard_map.50 = (bf16[64,512]{1,0:T(8,128)(2,1)S(1)}, bf16[64,512]{1,0:T(8,128)(2,1)S(1)}) custom-call(bf16[16,4,512]{2,1,0:T(4,128)(2,1)} %g_hbm.1, bf16[16,4,512]{2,1,0:T(4,128)(2,1)} %x_hbm.1, bf16[27,16,512]{2,1,0:T(8,128)(2,1)} %w_hbm.1), custom_call_target="tpu_custom_call" | custom-call | tf_op jit(solution)/shard_map/pallas_call | solution.py:444
  38.7 0.8 %copy_bitcast_fusion = (bf16[16,4,512]{2,1,0:T(4,128)(2,1)}, bf16[16,4,512]{2,1,0:T(4,128)(2,1)}) fusion(bf16[4,16,512]{2,1,0:T(8,128)(2,1)S(1)} %bitcast.6, bf16[4,16,512]{2,1,0:T(8,128)(2,1)S(1)} %bitcast.7), kind=kLoop, calls=%fused_computation | loop fusion | bytes 262144 | tf_op jit(solution)/shard_map/transpose | solution.py:482
